TPU v7x, 32 devices: a whole 2x2x4 slice. The times are simulated.
32 devices in a mesh: grp: 2 (over x), row: 16 (over z, y, core).
Axes of the slice: x: 2, y: 2, z: 4, core: 2. Of those that a mesh axis runs over, the one named last changes fastest.
Arguments:
- sources: bfloat16 [32, 8, 8, 1024], P(('grp', 'row')), parts along dimension 0, may hold values from -6 to 6
- far_left: bfloat16 [64, 15, 48, 1024], P(('grp', 'row')), parts along dimension 0, may hold values from -0.1875 to 0.1875
- far_right: bfloat16 [64, 15, 48, 1024], P(('grp', 'row')), parts along dimension 0, may hold values from -0.078125 to 0.078125
- ranks: int32 [64, 15], P(('grp', 'row')), parts along dimension 0, may hold values from 16 to 48
- near_blocks: bfloat16 [6, 1024, 1024], P('grp'), parts along dimension 0, may hold values from -0.1875 to 0.1875
- near_offsets: int32 [6, 2], P('grp'), parts along dimension 0, may hold values from -1 to 1, as said below
Outputs:
- fields: float32 [32, 8, 8, 1024], P(('grp', 'row')), parts along dimension 0
There are 2 independent parts, one for each index of `grp`. A program takes and returns all parts, laid end to end along the dimension named above; each array names one. Nothing has to cross between parts.
Inputs may be any that keep to these rules, and one draw needn't show every extreme that they name: `near_offsets`: the rows are 3 distinct offsets (a, b); row 0 is the self offset (0, 0).
All inputs are finite; a program needn't handle non-finite values.
Results may differ from a plain program's by a relative error of at most 0.0014.
Values may be sent and summed in bfloat16 or wider, within the bound.
A program may use at most 64 MiB of HBM per device.

v0:
```python
import jax
import jax.numpy as jnp
from jax import lax
from jax.sharding import PartitionSpec as P

RANK = 48
ECOL = 8
SLOTS = 15


def from_behind(value, axis, by):
    count = lax.axis_size(axis)
    return lax.ppermute(value, axis, [(i, (i + by) % count) for i in range(count)])


def padded_2(block, sides, width):
    for axis, dim in sides:
        count = lax.axis_size(axis)
        forward = [(i, i + 1) for i in range(count - 1)]
        backward = [(target, source) for source, target in forward]
        low = lax.ppermute(
            lax.slice_in_dim(block, block.shape[dim] - width, None, axis=dim), axis, forward
        )
        high = lax.ppermute(lax.slice_in_dim(block, 0, width, axis=dim), axis, backward)
        block = jnp.concatenate([low, block, high], axis=dim)
    return block


def slot_mask(rank_row, row_offset, near_offsets):
    col_offset = jnp.arange(SLOTS, dtype=jnp.int32) - (ECOL - 1)
    hit = jnp.any(
        (near_offsets[:, 0][:, None] == row_offset)
        & (near_offsets[:, 1][:, None] == col_offset[None, :]),
        axis=0,
    )
    live = jnp.arange(RANK, dtype=jnp.int32)[None, :] < rank_row[:, None]
    return (live & jnp.logical_not(hit)[:, None]).astype(jnp.float32)


def spread(coeffs):
    padded = jnp.pad(coeffs, ((ECOL, ECOL), (0, 0), (0, 0), (0, 0)))
    columns = [padded[2 * ECOL - 1 - k : 3 * ECOL - 1 - k, k, :, :] for k in range(SLOTS)]
    return jnp.stack(columns, axis=1)


def far_term(source_row, left, right, keep):
    coeffs = jnp.einsum("sbn,krn->skbr", source_row, left, preferred_element_type=jnp.float32)
    coeffs = (coeffs * keep[None, :, None, :]).astype(jnp.bfloat16)
    return jnp.einsum("jkbr,krn->jbn", spread(coeffs), right, preferred_element_type=jnp.float32)


def local(sources, far_left, far_right, ranks, near_blocks, near_offsets):
    cycle_size = lax.axis_size("row")
    place = lax.axis_index("row")
    keep_all = jnp.stack(
        [slot_mask(ranks[w], place - cycle_size * w, near_offsets) for w in range(2)], axis=0
    )
    ecol, beams, width = (sources.shape[1], sources.shape[2], sources.shape[3])

    def source_term(source_row, source_index):
        wrap_bit = (source_index + place >= cycle_size).astype(jnp.int32)
        left = lax.dynamic_index_in_dim(far_left, wrap_bit, 0, keepdims=False)
        right = lax.dynamic_index_in_dim(far_right, wrap_bit, 0, keepdims=False)
        keep = lax.dynamic_index_in_dim(keep_all, wrap_bit, 0, keepdims=False)
        return far_term(source_row, left, right, keep)

    gathered = lax.all_gather(sources, "row", axis=0, tiled=True)

    def step(source_index, accums):
        down_acc, up_acc = accums
        source_row = lax.dynamic_index_in_dim(gathered, source_index, 0, keepdims=False)
        down_acc = down_acc + source_term(source_row, source_index)
        down_acc = from_behind(down_acc, "row", -1)
        return (down_acc, up_acc)

    start = (jnp.zeros((ecol, beams, width), jnp.float32), jnp.zeros((1,), jnp.float32))
    far, unused_up = lax.fori_loop(0, cycle_size, step, start)
    beside = padded_2(sources, (("row", 0),), 1)
    beside = jnp.pad(beside, ((0, 0), (1, 1), (0, 0), (0, 0)))
    near = jnp.zeros((ecol * beams, width), jnp.float32)
    for index in range(near_blocks.shape[0]):
        row_offset = near_offsets[index, 0]
        col_offset = near_offsets[index, 1]
        anchor = (1 - row_offset, 1 - col_offset, jnp.int32(0), jnp.int32(0))
        shifted = lax.dynamic_slice(beside, anchor, (1, ecol, beams, width))
        near = near + jnp.dot(
            shifted.reshape(-1, width), near_blocks[index], preferred_element_type=jnp.float32
        )
    return (near.reshape(ecol, beams, width) + far).reshape(1, ecol, beams, width)


def solution(mesh):
    placed = (
        P(("grp", "row"), None, None, None),
        P(("grp", "row"), None, None, None),
        P(("grp", "row"), None, None, None),
        P(("grp", "row"), None),
        P("grp", None, None),
        P("grp", None),
    )
    return jax.shard_map(
        local,
        mesh=mesh,
        in_specs=placed,
        out_specs=P(("grp", "row"), None, None, None),
        check_vma=False,
    )
```

profile of v0, /device:TPU:0, one launch (start us, length us, event | category | flops | bytes accessed | tf_op | source)
XLA Modules:
  0.0 249.0 jit_solution(835424933795626141)
XLA Ops:
  29.0 24.7 %all-gather.2.cloned.1.call-done = bf16[16,8,8,1024]{3,2,1,0:T(8,128)(2,1)} async-done(((bf16[1,8,8,1024]{3,2,1,0:T(8,128)(2,1)}), bf16[16,8,8,1024]{3,2,1,0:T(8,128)(2,1)}) %all-gather.2.cloned.1.call-update) | async-done | bytes 2097168 | tf_op jit(solution)/shard_map/all_gather | solution.py:67
  53.7 185.6 %while.15 = (s32[]{:T(128)}, f32[8,8,1024]{2,1,0:T(8,128)S(1)}, s32[]{:T(128)}, bf16[2,15,48,1024]{3,2,1,0:T(8,128)(2,1)}, bf16[16,8,8,1024]{3,2,1,0:T(8,128)(2,...) while((s32[]{:T(128)}, f32[8,8,1024]{2,1,0:T(8,128)S(1)}, ...), condition=%wide.region_3.4_spmd, body=%wide.region_2.3_spmd.sunk | while | flops 188901376 | bytes 8549533 | solution.py:77
  59.0 3.9 %collective-permute-done = f32[8,8,1024]{2,1,0:T(8,128)S(1)} collective-permute-done((f32[8,8,1024]{2,1,0:T(8,128)S(1)}, f32[8,8,1024]{2,1,0:T(8,128)S(1)}, u32[]{:S(2)}, u32[]{:S(2)}) %collective-permute-start) | collective-permute-done | bytes 262176 | tf_op jit(solution)/shard_map/while/body/eval_jaxpr/ppermute | solution.py:13
  66.1 4.7 %collective-permute-start = (f32[8,8,1024]{2,1,0:T(8,128)S(1)}, f32[8,8,1024]{2,1,0:T(8,128)S(1)}, u32[]{:S(2)}, u32[]{:S(2)}) collective-permute-start(f32[8,8,1024]{2,1,0:T(8,128)S(1)} %fusion.81), channel_id=1, source_target_pairs={{0,15},{1,0},{2,1},{3,2},{4,3},{5,4},{6,5},{7,6},{8,7},{9,8},{10,9... | collective-permute-start | bytes 786440 | tf_op jit(solution)/shard_map/while/body/eval_jaxpr/ppermute | solution.py:13
  70.7 3.9 %collective-permute-done = f32[8,8,1024]{2,1,0:T(8,128)S(1)} collective-permute-done((f32[8,8,1024]{2,1,0:T(8,128)S(1)}, f32[8,8,1024]{2,1,0:T(8,128)S(1)}, u32[]{:S(2)}, u32[]{:S(2)}) %collective-permute-start) | collective-permute-done | bytes 262176 | tf_op jit(solution)/shard_map/while/body/eval_jaxpr/ppermute | solution.py:13
  77.8 4.7 %collective-permute-start = (f32[8,8,1024]{2,1,0:T(8,128)S(1)}, f32[8,8,1024]{2,1,0:T(8,128)S(1)}, u32[]{:S(2)}, u32[]{:S(2)}) collective-permute-start(f32[8,8,1024]{2,1,0:T(8,128)S(1)} %fusion.81), channel_id=1, source_target_pairs={{0,15},{1,0},{2,1},{3,2},{4,3},{5,4},{6,5},{7,6},{8,7},{9,8},{10,9... | collective-permute-start | bytes 786440 | tf_op jit(solution)/shard_map/while/body/eval_jaxpr/ppermute | solution.py:13
  82.5 3.9 %collective-permute-done = f32[8,8,1024]{2,1,0:T(8,128)S(1)} collective-permute-done((f32[8,8,1024]{2,1,0:T(8,128)S(1)}, f32[8,8,1024]{2,1,0:T(8,128)S(1)}, u32[]{:S(2)}, u32[]{:S(2)}) %collective-permute-start) | collective-permute-done | bytes 262176 | tf_op jit(solution)/shard_map/while/body/eval_jaxpr/ppermute | solution.py:13
  89.6 4.7 %collective-permute-start = (f32[8,8,1024]{2,1,0:T(8,128)S(1)}, f32[8,8,1024]{2,1,0:T(8,128)S(1)}, u32[]{:S(2)}, u32[]{:S(2)}) collective-permute-start(f32[8,8,1024]{2,1,0:T(8,128)S(1)} %fusion.81), channel_id=1, source_target_pairs={{0,15},{1,0},{2,1},{3,2},{4,3},{5,4},{6,5},{7,6},{8,7},{9,8},{10,9... | collective-permute-start | bytes 786440 | tf_op jit(solution)/shard_map/while/body/eval_jaxpr/ppermute | solution.py:13
  94.2 3.9 %collective-permute-done = f32[8,8,1024]{2,1,0:T(8,128)S(1)} collective-permute-done((f32[8,8,1024]{2,1,0:T(8,128)S(1)}, f32[8,8,1024]{2,1,0:T(8,128)S(1)}, u32[]{:S(2)}, u32[]{:S(2)}) %collective-permute-start) | collective-permute-done | bytes 262176 | tf_op jit(solution)/shard_map/while/body/eval_jaxpr/ppermute | solution.py:13
  101.4 4.7 %collective-permute-start = (f32[8,8,1024]{2,1,0:T(8,128)S(1)}, f32[8,8,1024]{2,1,0:T(8,128)S(1)}, u32[]{:S(2)}, u32[]{:S(2)}) collective-permute-start(f32[8,8,1024]{2,1,0:T(8,128)S(1)} %fusion.81), channel_id=1, source_target_pairs={{0,15},{1,0},{2,1},{3,2},{4,3},{5,4},{6,5},{7,6},{8,7},{9,8},{10,9... | collective-permute-start | bytes 786440 | tf_op jit(solution)/shard_map/while/body/eval_jaxpr/ppermute | solution.py:13
  106.0 3.9 %collective-permute-done = f32[8,8,1024]{2,1,0:T(8,128)S(1)} collective-permute-done((f32[8,8,1024]{2,1,0:T(8,128)S(1)}, f32[8,8,1024]{2,1,0:T(8,128)S(1)}, u32[]{:S(2)}, u32[]{:S(2)}) %collective-permute-start) | collective-permute-done | bytes 262176 | tf_op jit(solution)/shard_map/while/body/eval_jaxpr/ppermute | solution.py:13
  113.1 4.7 %collective-permute-start = (f32[8,8,1024]{2,1,0:T(8,128)S(1)}, f32[8,8,1024]{2,1,0:T(8,128)S(1)}, u32[]{:S(2)}, u32[]{:S(2)}) collective-permute-start(f32[8,8,1024]{2,1,0:T(8,128)S(1)} %fusion.81), channel_id=1, source_target_pairs={{0,15},{1,0},{2,1},{3,2},{4,3},{5,4},{6,5},{7,6},{8,7},{9,8},{10,9... | collective-permute-start | bytes 786440 | tf_op jit(solution)/shard_map/while/body/eval_jaxpr/ppermute | solution.py:13
  117.8 3.9 %collective-permute-done = f32[8,8,1024]{2,1,0:T(8,128)S(1)} collective-permute-done((f32[8,8,1024]{2,1,0:T(8,128)S(1)}, f32[8,8,1024]{2,1,0:T(8,128)S(1)}, u32[]{:S(2)}, u32[]{:S(2)}) %collective-permute-start) | collective-permute-done | bytes 262176 | tf_op jit(solution)/shard_map/while/body/eval_jaxpr/ppermute | solution.py:13
  124.9 4.7 %collective-permute-start = (f32[8,8,1024]{2,1,0:T(8,128)S(1)}, f32[8,8,1024]{2,1,0:T(8,128)S(1)}, u32[]{:S(2)}, u32[]{:S(2)}) collective-permute-start(f32[8,8,1024]{2,1,0:T(8,128)S(1)} %fusion.81), channel_id=1, source_target_pairs={{0,15},{1,0},{2,1},{3,2},{4,3},{5,4},{6,5},{7,6},{8,7},{9,8},{10,9... | collective-permute-start | bytes 786440 | tf_op jit(solution)/shard_map/while/body/eval_jaxpr/ppermute | solution.py:13
  129.5 3.9 %collective-permute-done = f32[8,8,1024]{2,1,0:T(8,128)S(1)} collective-permute-done((f32[8,8,1024]{2,1,0:T(8,128)S(1)}, f32[8,8,1024]{2,1,0:T(8,128)S(1)}, u32[]{:S(2)}, u32[]{:S(2)}) %collective-permute-start) | collective-permute-done | bytes 262176 | tf_op jit(solution)/shard_map/while/body/eval_jaxpr/ppermute | solution.py:13
  136.6 4.7 %collective-permute-start = (f32[8,8,1024]{2,1,0:T(8,128)S(1)}, f32[8,8,1024]{2,1,0:T(8,128)S(1)}, u32[]{:S(2)}, u32[]{:S(2)}) collective-permute-start(f32[8,8,1024]{2,1,0:T(8,128)S(1)} %fusion.81), channel_id=1, source_target_pairs={{0,15},{1,0},{2,1},{3,2},{4,3},{5,4},{6,5},{7,6},{8,7},{9,8},{10,9... | collective-permute-start | bytes 786440 | tf_op jit(solution)/shard_map/while/body/eval_jaxpr/ppermute | solution.py:13
  141.3 3.9 %collective-permute-done = f32[8,8,1024]{2,1,0:T(8,128)S(1)} collective-permute-done((f32[8,8,1024]{2,1,0:T(8,128)S(1)}, f32[8,8,1024]{2,1,0:T(8,128)S(1)}, u32[]{:S(2)}, u32[]{:S(2)}) %collective-permute-start) | collective-permute-done | bytes 262176 | tf_op jit(solution)/shard_map/while/body/eval_jaxpr/ppermute | solution.py:13
  148.4 4.7 %collective-permute-start = (f32[8,8,1024]{2,1,0:T(8,128)S(1)}, f32[8,8,1024]{2,1,0:T(8,128)S(1)}, u32[]{:S(2)}, u32[]{:S(2)}) collective-permute-start(f32[8,8,1024]{2,1,0:T(8,128)S(1)} %fusion.81), channel_id=1, source_target_pairs={{0,15},{1,0},{2,1},{3,2},{4,3},{5,4},{6,5},{7,6},{8,7},{9,8},{10,9... | collective-permute-start | bytes 786440 | tf_op jit(solution)/shard_map/while/body/eval_jaxpr/ppermute | solution.py:13
  153.1 3.9 %collective-permute-done = f32[8,8,1024]{2,1,0:T(8,128)S(1)} collective-permute-done((f32[8,8,1024]{2,1,0:T(8,128)S(1)}, f32[8,8,1024]{2,1,0:T(8,128)S(1)}, u32[]{:S(2)}, u32[]{:S(2)}) %collective-permute-start) | collective-permute-done | bytes 262176 | tf_op jit(solution)/shard_map/while/body/eval_jaxpr/ppermute | solution.py:13
  160.2 4.7 %collective-permute-start = (f32[8,8,1024]{2,1,0:T(8,128)S(1)}, f32[8,8,1024]{2,1,0:T(8,128)S(1)}, u32[]{:S(2)}, u32[]{:S(2)}) collective-permute-start(f32[8,8,1024]{2,1,0:T(8,128)S(1)} %fusion.81), channel_id=1, source_target_pairs={{0,15},{1,0},{2,1},{3,2},{4,3},{5,4},{6,5},{7,6},{8,7},{9,8},{10,9... | collective-permute-start | bytes 786440 | tf_op jit(solution)/shard_map/while/body/eval_jaxpr/ppermute | solution.py:13
  164.8 3.9 %collective-permute-done = f32[8,8,1024]{2,1,0:T(8,128)S(1)} collective-permute-done((f32[8,8,1024]{2,1,0:T(8,128)S(1)}, f32[8,8,1024]{2,1,0:T(8,128)S(1)}, u32[]{:S(2)}, u32[]{:S(2)}) %collective-permute-start) | collective-permute-done | bytes 262176 | tf_op jit(solution)/shard_map/while/body/eval_jaxpr/ppermute | solution.py:13
  171.9 4.7 %collective-permute-start = (f32[8,8,1024]{2,1,0:T(8,128)S(1)}, f32[8,8,1024]{2,1,0:T(8,128)S(1)}, u32[]{:S(2)}, u32[]{:S(2)}) collective-permute-start(f32[8,8,1024]{2,1,0:T(8,128)S(1)} %fusion.81), channel_id=1, source_target_pairs={{0,15},{1,0},{2,1},{3,2},{4,3},{5,4},{6,5},{7,6},{8,7},{9,8},{10,9... | collective-permute-start | bytes 786440 | tf_op jit(solution)/shard_map/while/body/eval_jaxpr/ppermute | solution.py:13
  176.6 3.9 %collective-permute-done = f32[8,8,1024]{2,1,0:T(8,128)S(1)} collective-permute-done((f32[8,8,1024]{2,1,0:T(8,128)S(1)}, f32[8,8,1024]{2,1,0:T(8,128)S(1)}, u32[]{:S(2)}, u32[]{:S(2)}) %collective-permute-start) | collective-permute-done | bytes 262176 | tf_op jit(solution)/shard_map/while/body/eval_jaxpr/ppermute | solution.py:13
  183.7 4.7 %collective-permute-start = (f32[8,8,1024]{2,1,0:T(8,128)S(1)}, f32[8,8,1024]{2,1,0:T(8,128)S(1)}, u32[]{:S(2)}, u32[]{:S(2)}) collective-permute-start(f32[8,8,1024]{2,1,0:T(8,128)S(1)} %fusion.81), channel_id=1, source_target_pairs={{0,15},{1,0},{2,1},{3,2},{4,3},{5,4},{6,5},{7,6},{8,7},{9,8},{10,9... | collective-permute-start | bytes 786440 | tf_op jit(solution)/shard_map/while/body/eval_jaxpr/ppermute | solution.py:13
  188.4 3.9 %collective-permute-done = f32[8,8,1024]{2,1,0:T(8,128)S(1)} collective-permute-done((f32[8,8,1024]{2,1,0:T(8,128)S(1)}, f32[8,8,1024]{2,1,0:T(8,128)S(1)}, u32[]{:S(2)}, u32[]{:S(2)}) %collective-permute-start) | collective-permute-done | bytes 262176 | tf_op jit(solution)/shard_map/while/body/eval_jaxpr/ppermute | solution.py:13
  195.5 4.7 %collective-permute-start = (f32[8,8,1024]{2,1,0:T(8,128)S(1)}, f32[8,8,1024]{2,1,0:T(8,128)S(1)}, u32[]{:S(2)}, u32[]{:S(2)}) collective-permute-start(f32[8,8,1024]{2,1,0:T(8,128)S(1)} %fusion.81), channel_id=1, source_target_pairs={{0,15},{1,0},{2,1},{3,2},{4,3},{5,4},{6,5},{7,6},{8,7},{9,8},{10,9... | collective-permute-start | bytes 786440 | tf_op jit(solution)/shard_map/while/body/eval_jaxpr/ppermute | solution.py:13
  200.1 3.9 %collective-permute-done = f32[8,8,1024]{2,1,0:T(8,128)S(1)} collective-permute-done((f32[8,8,1024]{2,1,0:T(8,128)S(1)}, f32[8,8,1024]{2,1,0:T(8,128)S(1)}, u32[]{:S(2)}, u32[]{:S(2)}) %collective-permute-start) | collective-permute-done | bytes 262176 | tf_op jit(solution)/shard_map/while/body/eval_jaxpr/ppermute | solution.py:13
  207.2 4.7 %collective-permute-start = (f32[8,8,1024]{2,1,0:T(8,128)S(1)}, f32[8,8,1024]{2,1,0:T(8,128)S(1)}, u32[]{:S(2)}, u32[]{:S(2)}) collective-permute-start(f32[8,8,1024]{2,1,0:T(8,128)S(1)} %fusion.81), channel_id=1, source_target_pairs={{0,15},{1,0},{2,1},{3,2},{4,3},{5,4},{6,5},{7,6},{8,7},{9,8},{10,9... | collective-permute-start | bytes 786440 | tf_op jit(solution)/shard_map/while/body/eval_jaxpr/ppermute | solution.py:13
  211.9 3.9 %collective-permute-done = f32[8,8,1024]{2,1,0:T(8,128)S(1)} collective-permute-done((f32[8,8,1024]{2,1,0:T(8,128)S(1)}, f32[8,8,1024]{2,1,0:T(8,128)S(1)}, u32[]{:S(2)}, u32[]{:S(2)}) %collective-permute-start) | collective-permute-done | bytes 262176 | tf_op jit(solution)/shard_map/while/body/eval_jaxpr/ppermute | solution.py:13
  219.0 4.7 %collective-permute-start = (f32[8,8,1024]{2,1,0:T(8,128)S(1)}, f32[8,8,1024]{2,1,0:T(8,128)S(1)}, u32[]{:S(2)}, u32[]{:S(2)}) collective-permute-start(f32[8,8,1024]{2,1,0:T(8,128)S(1)} %fusion.81), channel_id=1, source_target_pairs={{0,15},{1,0},{2,1},{3,2},{4,3},{5,4},{6,5},{7,6},{8,7},{9,8},{10,9... | collective-permute-start | bytes 786440 | tf_op jit(solution)/shard_map/while/body/eval_jaxpr/ppermute | solution.py:13
  223.7 3.9 %collective-permute-done = f32[8,8,1024]{2,1,0:T(8,128)S(1)} collective-permute-done((f32[8,8,1024]{2,1,0:T(8,128)S(1)}, f32[8,8,1024]{2,1,0:T(8,128)S(1)}, u32[]{:S(2)}, u32[]{:S(2)}) %collective-permute-start) | collective-permute-done | bytes 262176 | tf_op jit(solution)/shard_map/while/body/eval_jaxpr/ppermute | solution.py:13
  230.8 4.7 %collective-permute-start = (f32[8,8,1024]{2,1,0:T(8,128)S(1)}, f32[8,8,1024]{2,1,0:T(8,128)S(1)}, u32[]{:S(2)}, u32[]{:S(2)}) collective-permute-start(f32[8,8,1024]{2,1,0:T(8,128)S(1)} %fusion.81), channel_id=1, source_target_pairs={{0,15},{1,0},{2,1},{3,2},{4,3},{5,4},{6,5},{7,6},{8,7},{9,8},{10,9... | collective-permute-start | bytes 786440 | tf_op jit(solution)/shard_map/while/body/eval_jaxpr/ppermute | solution.py:13
  (315 shorter events, 74.2 us)
Async XLA Ops:
  6.5 47.1 %all-gather.2.cloned.1.call-start = ((), (), s32[]{:S(2)}) async-start(), calls=%async_computation | async-start | bytes 2228224 | tf_op jit(solution)/shard_map/all_gather | solution.py:67
  7.3 14.9 %collective-permute-start.1 = (bf16[1,8,8,1024]{3,2,1,0:T(8,128)(2,1)}, bf16[1,8,8,1024]{3,2,1,0:T(8,128)(2,1)S(1)}, u32[]{:S(2)}, u32[]{:S(2)}) collective-permute-start(bf16[1,8,8,1024]{3,2,1,0:T(8,128)(2,1)} %param.8), channel_id=1, source_target_pairs={{0,1},{1,2},{2,3},{3,4},{4,5},{5,6},{6,7},{7,8},{8,9},{9,10},{10,1... | collective-permute-start | bytes 393224 | tf_op jit(solution)/shard_map/ppermute | solution.py:21
  9.6 12.5 %collective-permute-start.2 = (bf16[1,8,8,1024]{3,2,1,0:T(8,128)(2,1)}, bf16[1,8,8,1024]{3,2,1,0:T(8,128)(2,1)S(1)}, u32[]{:S(2)}, u32[]{:S(2)}) collective-permute-start(bf16[1,8,8,1024]{3,2,1,0:T(8,128)(2,1)} %param.8), channel_id=1, source_target_pairs={{1,0},{2,1},{3,2},{4,3},{5,4},{6,5},{7,6},{8,7},{9,8},{10,9},{11,1... | collective-permute-start | bytes 393224 | tf_op jit(solution)/shard_map/ppermute | solution.py:24
  22.1 31.6 %copy-start = (bf16[2,15,48,1024]{3,2,1,0:T(8,128)(2,1)S(1)}, bf16[2,15,48,1024]{3,2,1,0:T(8,128)(2,1)}, u32[]{:S(2)}) copy-start(bf16[2,15,48,1024]{3,2,1,0:T(8,128)(2,1)} %param.10) | copy-start | bytes 8847364
  23.3 3.0 %copy-start.1 = (bf16[3,10,8,1024]{3,2,1,0:T(8,128)(2,1)}, bf16[3,10,8,1024]{3,2,1,0:T(8,128)(2,1)S(1)}, u32[]{:S(2)}) copy-start(bf16[3,10,8,1024]{3,2,1,0:T(8,128)(2,1)S(1)} %fusion.54) | copy-start | bytes 1474564
  57.0 5.9 %collective-permute-start = (f32[8,8,1024]{2,1,0:T(8,128)S(1)}, f32[8,8,1024]{2,1,0:T(8,128)S(1)}, u32[]{:S(2)}, u32[]{:S(2)}) collective-permute-start(f32[8,8,1024]{2,1,0:T(8,128)S(1)} %fusion.81), channel_id=1, source_target_pairs={{0,15},{1,0},{2,1},{3,2},{4,3},{5,4},{6,5},{7,6},{8,7},{9,8},{10,9... | collective-permute-start | bytes 786440 | tf_op jit(solution)/shard_map/while/body/eval_jaxpr/ppermute | solution.py:13
  66.1 8.5 %collective-permute-start = (f32[8,8,1024]{2,1,0:T(8,128)S(1)}, f32[8,8,1024]{2,1,0:T(8,128)S(1)}, u32[]{:S(2)}, u32[]{:S(2)}) collective-permute-start(f32[8,8,1024]{2,1,0:T(8,128)S(1)} %fusion.81), channel_id=1, source_target_pairs={{0,15},{1,0},{2,1},{3,2},{4,3},{5,4},{6,5},{7,6},{8,7},{9,8},{10,9... | collective-permute-start | bytes 786440 | tf_op jit(solution)/shard_map/while/body/eval_jaxpr/ppermute | solution.py:13
  77.8 8.5 %collective-permute-start = (f32[8,8,1024]{2,1,0:T(8,128)S(1)}, f32[8,8,1024]{2,1,0:T(8,128)S(1)}, u32[]{:S(2)}, u32[]{:S(2)}) collective-permute-start(f32[8,8,1024]{2,1,0:T(8,128)S(1)} %fusion.81), channel_id=1, source_target_pairs={{0,15},{1,0},{2,1},{3,2},{4,3},{5,4},{6,5},{7,6},{8,7},{9,8},{10,9... | collective-permute-start | bytes 786440 | tf_op jit(solution)/shard_map/while/body/eval_jaxpr/ppermute | solution.py:13
  89.6 8.5 %collective-permute-start = (f32[8,8,1024]{2,1,0:T(8,128)S(1)}, f32[8,8,1024]{2,1,0:T(8,128)S(1)}, u32[]{:S(2)}, u32[]{:S(2)}) collective-permute-start(f32[8,8,1024]{2,1,0:T(8,128)S(1)} %fusion.81), channel_id=1, source_target_pairs={{0,15},{1,0},{2,1},{3,2},{4,3},{5,4},{6,5},{7,6},{8,7},{9,8},{10,9... | collective-permute-start | bytes 786440 | tf_op jit(solution)/shard_map/while/body/eval_jaxpr/ppermute | solution.py:13
  101.4 8.5 %collective-permute-start = (f32[8,8,1024]{2,1,0:T(8,128)S(1)}, f32[8,8,1024]{2,1,0:T(8,128)S(1)}, u32[]{:S(2)}, u32[]{:S(2)}) collective-permute-start(f32[8,8,1024]{2,1,0:T(8,128)S(1)} %fusion.81), channel_id=1, source_target_pairs={{0,15},{1,0},{2,1},{3,2},{4,3},{5,4},{6,5},{7,6},{8,7},{9,8},{10,9... | collective-permute-start | bytes 786440 | tf_op jit(solution)/shard_map/while/body/eval_jaxpr/ppermute | solution.py:13
  113.1 8.5 %collective-permute-start = (f32[8,8,1024]{2,1,0:T(8,128)S(1)}, f32[8,8,1024]{2,1,0:T(8,128)S(1)}, u32[]{:S(2)}, u32[]{:S(2)}) collective-permute-start(f32[8,8,1024]{2,1,0:T(8,128)S(1)} %fusion.81), channel_id=1, source_target_pairs={{0,15},{1,0},{2,1},{3,2},{4,3},{5,4},{6,5},{7,6},{8,7},{9,8},{10,9... | collective-permute-start | bytes 786440 | tf_op jit(solution)/shard_map/while/body/eval_jaxpr/ppermute | solution.py:13
  124.9 8.5 %collective-permute-start = (f32[8,8,1024]{2,1,0:T(8,128)S(1)}, f32[8,8,1024]{2,1,0:T(8,128)S(1)}, u32[]{:S(2)}, u32[]{:S(2)}) collective-permute-start(f32[8,8,1024]{2,1,0:T(8,128)S(1)} %fusion.81), channel_id=1, source_target_pairs={{0,15},{1,0},{2,1},{3,2},{4,3},{5,4},{6,5},{7,6},{8,7},{9,8},{10,9... | collective-permute-start | bytes 786440 | tf_op jit(solution)/shard_map/while/body/eval_jaxpr/ppermute | solution.py:13
  136.6 8.5 %collective-permute-start = (f32[8,8,1024]{2,1,0:T(8,128)S(1)}, f32[8,8,1024]{2,1,0:T(8,128)S(1)}, u32[]{:S(2)}, u32[]{:S(2)}) collective-permute-start(f32[8,8,1024]{2,1,0:T(8,128)S(1)} %fusion.81), channel_id=1, source_target_pairs={{0,15},{1,0},{2,1},{3,2},{4,3},{5,4},{6,5},{7,6},{8,7},{9,8},{10,9... | collective-permute-start | bytes 786440 | tf_op jit(solution)/shard_map/while/body/eval_jaxpr/ppermute | solution.py:13
  148.4 8.5 %collective-permute-start = (f32[8,8,1024]{2,1,0:T(8,128)S(1)}, f32[8,8,1024]{2,1,0:T(8,128)S(1)}, u32[]{:S(2)}, u32[]{:S(2)}) collective-permute-start(f32[8,8,1024]{2,1,0:T(8,128)S(1)} %fusion.81), channel_id=1, source_target_pairs={{0,15},{1,0},{2,1},{3,2},{4,3},{5,4},{6,5},{7,6},{8,7},{9,8},{10,9... | collective-permute-start | bytes 786440 | tf_op jit(solution)/shard_map/while/body/eval_jaxpr/ppermute | solution.py:13
  160.2 8.5 %collective-permute-start = (f32[8,8,1024]{2,1,0:T(8,128)S(1)}, f32[8,8,1024]{2,1,0:T(8,128)S(1)}, u32[]{:S(2)}, u32[]{:S(2)}) collective-permute-start(f32[8,8,1024]{2,1,0:T(8,128)S(1)} %fusion.81), channel_id=1, source_target_pairs={{0,15},{1,0},{2,1},{3,2},{4,3},{5,4},{6,5},{7,6},{8,7},{9,8},{10,9... | collective-permute-start | bytes 786440 | tf_op jit(solution)/shard_map/while/body/eval_jaxpr/ppermute | solution.py:13
  171.9 8.5 %collective-permute-start = (f32[8,8,1024]{2,1,0:T(8,128)S(1)}, f32[8,8,1024]{2,1,0:T(8,128)S(1)}, u32[]{:S(2)}, u32[]{:S(2)}) collective-permute-start(f32[8,8,1024]{2,1,0:T(8,128)S(1)} %fusion.81), channel_id=1, source_target_pairs={{0,15},{1,0},{2,1},{3,2},{4,3},{5,4},{6,5},{7,6},{8,7},{9,8},{10,9... | collective-permute-start | bytes 786440 | tf_op jit(solution)/shard_map/while/body/eval_jaxpr/ppermute | solution.py:13
  183.7 8.5 %collective-permute-start = (f32[8,8,1024]{2,1,0:T(8,128)S(1)}, f32[8,8,1024]{2,1,0:T(8,128)S(1)}, u32[]{:S(2)}, u32[]{:S(2)}) collective-permute-start(f32[8,8,1024]{2,1,0:T(8,128)S(1)} %fusion.81), channel_id=1, source_target_pairs={{0,15},{1,0},{2,1},{3,2},{4,3},{5,4},{6,5},{7,6},{8,7},{9,8},{10,9... | collective-permute-start | bytes 786440 | tf_op jit(solution)/shard_map/while/body/eval_jaxpr/ppermute | solution.py:13
  195.5 8.5 %collective-permute-start = (f32[8,8,1024]{2,1,0:T(8,128)S(1)}, f32[8,8,1024]{2,1,0:T(8,128)S(1)}, u32[]{:S(2)}, u32[]{:S(2)}) collective-permute-start(f32[8,8,1024]{2,1,0:T(8,128)S(1)} %fusion.81), channel_id=1, source_target_pairs={{0,15},{1,0},{2,1},{3,2},{4,3},{5,4},{6,5},{7,6},{8,7},{9,8},{10,9... | collective-permute-start | bytes 786440 | tf_op jit(solution)/shard_map/while/body/eval_jaxpr/ppermute | solution.py:13
  207.2 8.5 %collective-permute-start = (f32[8,8,1024]{2,1,0:T(8,128)S(1)}, f32[8,8,1024]{2,1,0:T(8,128)S(1)}, u32[]{:S(2)}, u32[]{:S(2)}) collective-permute-start(f32[8,8,1024]{2,1,0:T(8,128)S(1)} %fusion.81), channel_id=1, source_target_pairs={{0,15},{1,0},{2,1},{3,2},{4,3},{5,4},{6,5},{7,6},{8,7},{9,8},{10,9... | collective-permute-start | bytes 786440 | tf_op jit(solution)/shard_map/while/body/eval_jaxpr/ppermute | solution.py:13
  219.0 8.5 %collective-permute-start = (f32[8,8,1024]{2,1,0:T(8,128)S(1)}, f32[8,8,1024]{2,1,0:T(8,128)S(1)}, u32[]{:S(2)}, u32[]{:S(2)}) collective-permute-start(f32[8,8,1024]{2,1,0:T(8,128)S(1)} %fusion.81), channel_id=1, source_target_pairs={{0,15},{1,0},{2,1},{3,2},{4,3},{5,4},{6,5},{7,6},{8,7},{9,8},{10,9... | collective-permute-start | bytes 786440 | tf_op jit(solution)/shard_map/while/body/eval_jaxpr/ppermute | solution.py:13
  230.8 8.5 %collective-permute-start = (f32[8,8,1024]{2,1,0:T(8,128)S(1)}, f32[8,8,1024]{2,1,0:T(8,128)S(1)}, u32[]{:S(2)}, u32[]{:S(2)}) collective-permute-start(f32[8,8,1024]{2,1,0:T(8,128)S(1)} %fusion.81), channel_id=1, source_target_pairs={{0,15},{1,0},{2,1},{3,2},{4,3},{5,4},{6,5},{7,6},{8,7},{9,8},{10,9... | collective-permute-start | bytes 786440 | tf_op jit(solution)/shard_map/while/body/eval_jaxpr/ppermute | solution.py:13
Sparse Core Ops, SparseCore 0:
  9.5 44.1 all-gather.1
where the time goes:
time: 250 us; the launch traced here: 249 us
  waiting for transfers between devices  87.6 us (35%)
  starting transfers between devices  75.5 us (30%)
  matrix products  55.8 us (22%)
  between operations  20.8 us (8%)
  local copies, waits for them, and re-layouts  6.14 us (2%)
    ppermute x16, starting transfers between devices, from_behind(): lax.ppermute(value, axis, [(i, (i + by) % count) for i in range(count)])  71.9 us
    ppermute x16, waiting for transfers between devices, from_behind(): lax.ppermute(value, axis, [(i, (i + by) % count) for i in range(count)])  62.2 us
    dot_general x16, matrix products, far_term(): jnp.einsum('sbn,krn->skbr', source_row, left, preferred_element_type=jnp....  37.4 us
    all_gather x1, waiting for transfers between devices, local(): gathered = lax.all_gather(sources, 'row', axis=0, tiled=True)  24.7 us
    dot_general x16, matrix products, far_term(): jnp.einsum('jkbr,krn->jbn', spread(coeffs), right, preferred_element_type...  9.73 us
    dot_general x3, matrix products, local(): jnp.dot(shifted.reshape(-1, width), near_blocks[index], preferred_element...  8.65 us
  transfers between devices with their start and end apart: 19, of which 17 were waited for; matrix products, arithmetic and copies ran while one was open for 4% of the time, Pallas kernels for 0%

commit v1 on v0

v1 whole, which is shorter than its diff:
```python
import functools

import jax
import jax.numpy as jnp
from jax import lax
from jax.experimental import pallas as pl
from jax.experimental.pallas import tpu as pltpu
from jax.sharding import PartitionSpec as P

MESH = pl.DeviceIdType.MESH
F32 = jnp.float32
BF16 = jnp.bfloat16
LANES = 128


def kernel(
    dims,
    src, left_hbm, right_hbm, near_hbm, ranks, offsets,
    out,
    rows_all, left, right, near_w, coeff_pad, spread_all, partial, sib_in,
    ring_out, ring_in, beside, keep, near_acc,
    load_sem, g_send, g_recv, gs_send, gs_recv, r_send, r_recv, rs_send, rs_recv,
):
    count, ecol, beams, width, slots, rank, depth, nnear = dims
    chips = count // 2
    half_ring = chips // 2
    rows = ecol * beams
    half = rows // 2
    used = slots * rank

    me = lax.axis_index("row")
    core = me % 2
    chip = me // 2
    pos = (1 - chip % 2) * (chip // 2) + (chip % 2) * (chips - 1 - chip // 2)

    def chip_at(place):
        place = (place + 2 * chips) % chips
        upper = place // half_ring
        return (1 - upper) * 2 * place + upper * (2 * (chips - 1 - place) + 1)

    def row_at(place):
        return 2 * chip_at(place) + core

    ahead = row_at(pos + 1)
    behind = row_at(pos - 1)
    sibling = me + 1 - 2 * core

    def send(source, target, send_sem, recv_sem, device):
        return pltpu.make_async_remote_copy(
            src_ref=source, dst_ref=target, send_sem=send_sem, recv_sem=recv_sem,
            device_id={"row": device}, device_id_type=MESH,
        )

    loads = [pltpu.make_async_copy(src, rows_all.at[me], load_sem.at[0])]
    for w in range(2):
        loads.append(pltpu.make_async_copy(
            left_hbm.at[w], left.at[w, pl.ds(0, used)], load_sem.at[1 + w]))
        loads.append(pltpu.make_async_copy(
            right_hbm.at[w], right.at[w, pl.ds(0, used)], load_sem.at[3 + w]))
    loads.append(pltpu.make_async_copy(near_hbm, near_w, load_sem.at[5]))

    barrier = pltpu.get_barrier_semaphore()
    for device in (ahead, behind, sibling):
        pl.semaphore_signal(barrier, inc=1, device_id={"row": device}, device_id_type=MESH)
    loads[0].start()
    loads[1].start()
    loads[3].start()
    pl.semaphore_wait(barrier, 3)

    def part(ref, lead, h):
        return ref.at[lead, pl.ds(h * half, half)]

    def hop(way, step, h, row, source=None):
        block = part(rows_all, row, h)
        return send(
            block if source is None else source, block,
            g_send.at[way, step - 1, h], g_recv.at[way, step - 1, h],
            ahead if way == 0 else behind,
        )

    def cross(index, h, row, source=None):
        block = part(rows_all, row, h)
        return send(
            block if source is None else source, block,
            gs_send.at[index, h], gs_recv.at[index, h], sibling,
        )

    for h in range(2):
        mine = src.at[pl.ds(h * half, half)]
        hop(0, 1, h, me, mine).start()
        hop(1, 1, h, me, mine).start()
        cross(0, h, me, mine).start()
    loads[2].start()
    loads[4].start()
    loads[5].start()

    for w in range(2):
        left[w, pl.ds(used, depth - used), :] = jnp.zeros((depth - used, width), BF16)
        right[w, pl.ds(used, depth - used), :] = jnp.zeros((depth - used, width), BF16)
    for i in range(2):
        coeff_pad[i, pl.ds(0, rows), :] = jnp.zeros((rows, depth), F32)
        coeff_pad[i, pl.ds(2 * rows, rows), :] = jnp.zeros((rows, depth), F32)
    lane = lax.broadcasted_iota(jnp.int32, (8, depth), 1)
    for w in range(2):
        top = jnp.zeros((8, depth), jnp.int32)
        for k in range(slots):
            free = jnp.int32(1)
            for n in range(nnear):
                rows_off = offsets[n, 0] - (me - count * w)
                cols_off = offsets[n, 1] - (k - (ecol - 1))
                free = free * jnp.minimum(rows_off * rows_off + cols_off * cols_off, 1)
            level = rank * k + ranks[w, k] * free
            top = jnp.where(lane >= rank * k, level, top)
        top = jnp.where(lane < used, top, 0)
        keep[w] = jnp.clip(top - lane, 0, 1).astype(F32)

    tile_lane = lax.broadcasted_iota(jnp.int32, (rows, LANES), 1)

    def wrap(source):
        return (source + me) // count

    def coeffs_of(place):
        first = 2 * chip_at(place)
        block = rows_all[pl.ds(first, 2)].reshape(2 * rows, width)

        def one(w, carry):
            product = lax.dot_general(
                block, left[w], (((1,), (1,)), ((), ())), preferred_element_type=F32)
            mask = keep[w][0:1, :]
            for i in range(2):
                @pl.when(wrap(first + i) == w)
                def _():
                    coeff_pad[i, pl.ds(rows, rows), :] = (
                        product[i * rows:(i + 1) * rows, :] * mask)
            return carry

        lax.fori_loop(wrap(first), wrap(first + 1) + 1, one, 0)
        for i in range(2):
            target = (first + i + me) % count
            for tile in range(depth // LANES):
                low = tile * LANES
                first_k = min(low // rank, slots - 1)
                last_k = min((low + LANES - 1) // rank, slots - 1)
                value = None
                for k in range(first_k, last_k + 1):
                    start = rows + (ecol - 1 - k) * beams
                    piece = coeff_pad[i, pl.ds(start, rows), pl.ds(low, LANES)]
                    if value is None:
                        value = piece
                    else:
                        value = jnp.where(tile_lane >= rank * k - low, piece, value)
                spread_all[target, :, pl.ds(low, LANES)] = value.astype(BF16)

    def take(step, all_on):
        for h in range(2):
            for way in range(2):
                row = row_at(pos - step if way == 0 else pos + step)
                index = chips - step if way == 0 else step
                hop(way, step, h, row).wait_recv()
                if all_on or h == way:
                    hop(way, step + 1, h, row).start()
                cross(index, h, row).start()

    def cross_arrived(index, place):
        other = 2 * chip_at(place) + 1 - core
        for h in range(2):
            cross(index, h, other).wait_recv()

    def both_coeffs(step):
        def one(way, carry):
            index = (1 - way) * (chips - step) + way * step
            cross_arrived(index, pos + index)
            coeffs_of(pos + index)
            return carry
        lax.fori_loop(0, 2, one, 0)

    def gather_step(step, carry):
        take(step, True)

        @pl.when(step == 1)
        def _():
            loads[0].wait()
            loads[1].wait()
            loads[3].wait()
            cross_arrived(0, pos)
            coeffs_of(pos)

        @pl.when(step > 1)
        def _():
            both_coeffs(step - 1)
        return carry

    lax.fori_loop(1, half_ring - 1, gather_step, 0)
    take(half_ring - 1, False)
    both_coeffs(half_ring - 2)
    for way in range(2):
        hop(way, half_ring, way, row_at(pos + half_ring)).wait_recv()
        cross(half_ring, way, row_at(pos + half_ring)).start()
    both_coeffs(half_ring - 1)
    cross_arrived(half_ring, pos + half_ring)
    coeffs_of(pos + half_ring)

    def behind_me(target):
        return (target < me).astype(jnp.int32)

    def cross_sum(index):
        return send(
            partial.at[index, 1 - core], sib_in.at[index],
            rs_send.at[index], rs_recv.at[index], sibling)

    def fields_of(index):
        first = 2 * chip_at(pos + index)
        block = spread_all[pl.ds(first, 2)].reshape(2 * rows, depth)

        def one(w, carry):
            product = jnp.dot(block, right[w], preferred_element_type=F32)
            for i in range(2):
                @pl.when(behind_me(first + i) == w)
                def _():
                    partial[index, i] = product[i * rows:(i + 1) * rows, :]
            return carry

        lax.fori_loop(behind_me(first + 1), behind_me(first) + 1, one, 0)
        cross_sum(index).start()

    def both_fields(distance):
        def one(way, carry):
            fields_of((1 - way) * distance + way * (chips - distance))
            return carry
        lax.fori_loop(0, 2, one, 0)

    def ring(way, step, h):
        return send(
            ring_out.at[way, step - 1, pl.ds(h * half, half)],
            ring_in.at[way, step - 1, pl.ds(h * half, half)],
            r_send.at[way, step - 1, h], r_recv.at[way, step - 1, h],
            ahead if way == 0 else behind,
        )

    def own(index, h):
        at = pl.ds(h * half, half)
        return partial[index, core, at, :] + sib_in[index, at, :]

    def pass_on(step, way, h, fresh):
        distance = half_ring - (step - 1)
        index = distance if way == 0 else chips - distance
        at = pl.ds(h * half, half)
        total = own(index, h)
        if not fresh:
            ring(way, step - 1, h).wait_recv()
            total = total + ring_in[way, step - 2, at, :].astype(F32)
        ring_out[way, step - 1, at, :] = total.astype(ring_out.dtype)
        ring(way, step, h).start()

    loads[2].wait()
    loads[4].wait()
    fields_of(half_ring)
    both_fields(half_ring - 1)
    cross_sum(half_ring).wait_recv()
    pass_on(1, 0, 0, True)
    pass_on(1, 1, 1, True)
    cross_sum(half_ring - 1).wait_recv()
    cross_sum(chips - half_ring + 1).wait_recv()
    pass_on(2, 0, 1, True)
    pass_on(2, 1, 0, True)
    both_fields(half_ring - 2)
    pass_on(2, 0, 0, False)
    pass_on(2, 1, 1, False)

    def reduce_step(step, carry):
        distance = half_ring - step

        @pl.when(distance > 0)
        def _():
            both_fields(distance)
        cross_sum(distance + 1).wait_recv()
        cross_sum(chips - distance - 1).wait_recv()
        pass_on(step, 0, 1, False)
        pass_on(step, 1, 0, False)
        pass_on(step, 0, 0, False)
        pass_on(step, 1, 1, False)
        return carry

    lax.fori_loop(3, half_ring + 1, reduce_step, 0)
    fields_of(0)

    loads[5].wait()
    for i in range(3):
        row = me + i - 1
        inside = jnp.logical_and(row >= 0, row < count)
        block = rows_all[(row + count) % count].astype(F32)
        beside[i, pl.ds(0, beams), :] = jnp.zeros((beams, width), F32)
        beside[i, pl.ds(beams, rows), :] = jnp.where(inside, block, 0.0)
        beside[i, pl.ds(beams + rows, beams), :] = jnp.zeros((beams, width), F32)
    near_acc[...] = jnp.zeros((rows, width), F32)

    def weights(offset):
        square = offset * offset
        return [((square + offset) // 2).astype(F32), (1 - square).astype(F32),
                ((square - offset) // 2).astype(F32)]

    def near_step(n, carry):
        by_row = weights(offsets[n, 0])
        by_col = weights(offsets[n, 1])
        picked = sum(beside[i] * by_row[i] for i in range(3))
        shifted = sum(
            picked[i * beams:i * beams + rows, :] * by_col[i] for i in range(3)).astype(BF16)
        near_acc[...] += jnp.dot(shifted, near_w[n], preferred_element_type=F32)
        return carry

    lax.fori_loop(0, nnear, near_step, 0)

    cross_sum(0).wait_recv()
    for h in range(2):
        at = pl.ds(h * half, half)
        total = near_acc[at, :] + own(0, h)
        for way in range(2):
            ring(way, half_ring, h).wait_recv()
            total = total + ring_in[way, half_ring - 1, at, :].astype(F32)
        out[at, :] = total

    def sent(step, carry):
        for way in range(2):
            for h in range(2):
                hop(way, step, h, me).wait_send()
                ring(way, half_ring + 1 - step, h).wait_send()
        return carry

    lax.fori_loop(1, half_ring, sent, 0)
    for way in range(2):
        hop(way, half_ring, way, me).wait_send()
        ring(way, 1, way).wait_send()

    def crossed(index, carry):
        for h in range(2):
            cross(index, h, me).wait_send()
        cross_sum(index).wait_send()
        return carry

    lax.fori_loop(0, chips, crossed, 0)


def local(count, sources, far_left, far_right, ranks, near_blocks, near_offsets):
    _, ecol, beams, width = sources.shape
    slots, rank = far_left.shape[1], far_left.shape[2]
    nnear = near_blocks.shape[0]
    chips, rows = count // 2, ecol * beams
    half_ring = chips // 2
    depth = -(-slots * rank // 256) * 256
    dims = (count, ecol, beams, width, slots, rank, depth, nnear)
    flops = 2 * count * rows * depth * width * 2 + 2 * nnear * rows * width * width
    dma = pltpu.SemaphoreType.DMA
    anywhere = pl.BlockSpec(memory_space=pl.ANY)
    scalars = pl.BlockSpec(memory_space=pltpu.SMEM)
    fields = pl.pallas_call(
        functools.partial(kernel, dims),
        out_shape=jax.ShapeDtypeStruct((rows, width), F32),
        in_specs=[anywhere] * 4 + [scalars] * 2,
        out_specs=pl.BlockSpec(memory_space=pltpu.VMEM),
        scratch_shapes=[
            pltpu.VMEM((count, rows, width), BF16),
            pltpu.VMEM((2, depth, width), BF16),
            pltpu.VMEM((2, depth, width), BF16),
            pltpu.VMEM((nnear, width, width), BF16),
            pltpu.VMEM((2, 3 * rows, depth), F32),
            pltpu.VMEM((count, rows, depth), BF16),
            pltpu.VMEM((chips, 2, rows, width), F32),
            pltpu.VMEM((chips, rows, width), F32),
            pltpu.VMEM((2, half_ring, rows, width), BF16),
            pltpu.VMEM((2, half_ring, rows, width), BF16),
            pltpu.VMEM((3, rows + 2 * beams, width), F32),
            pltpu.VMEM((2, 8, depth), F32),
            pltpu.VMEM((rows, width), F32),
            dma((6,)),
            dma((2, half_ring, 2)),
            dma((2, half_ring, 2)),
            dma((chips, 2)),
            dma((chips, 2)),
            dma((2, half_ring, 2)),
            dma((2, half_ring, 2)),
            dma((chips,)),
            dma((chips,)),
        ],
        compiler_params=pltpu.CompilerParams(
            collective_id=0, has_side_effects=True, vmem_limit_bytes=62 * 2 ** 20),
        cost_estimate=pl.CostEstimate(
            flops=flops, bytes_accessed=13_000_000, transcendentals=0),
    )(
        sources.reshape(rows, width),
        far_left.reshape(2, slots * rank, width),
        far_right.reshape(2, slots * rank, width),
        near_blocks, ranks, near_offsets,
    )
    return fields.reshape(1, ecol, beams, width)


def solution(mesh):
    placed = (
        P(("grp", "row"), None, None, None),
        P(("grp", "row"), None, None, None),
        P(("grp", "row"), None, None, None),
        P(("grp", "row"), None),
        P("grp", None, None),
        P("grp", None),
    )
    return jax.shard_map(
        functools.partial(local, mesh.shape["row"]),
        mesh=mesh,
        in_specs=placed,
        out_specs=P(("grp", "row"), None, None, None),
        check_vma=False,
    )
```

time: 250 us -> 45.2 us (0.18)
  waiting for transfers between devices: 87.6 us -> 0 us
  starting transfers between devices: 75.5 us -> 0 us
  matrix products: 55.8 us -> 0 us
  Pallas kernels: 0 us -> 42 us
  between operations: 20.8 us -> 0.01 us
  local copies, waits for them, and re-layouts: 6.14 us -> 3.01 us
    ppermute x18 -> x0, starting transfers between devices: 75.5 us -> none  [the longest x16 71.9 us: from_behind(): lax.ppermute(value, axis, [(i, (i + by) % count) for i in range(count)])]
    ppermute x18 -> x0, waiting for transfers between devices: 62.3 us -> none  [the longest x16 62.2 us: from_behind(): lax.ppermute(value, axis, [(i, (i + by) % count) for i in range(count)])]
    dot_general x35 -> x0, matrix products: 55.8 us -> none  [the longest x16 37.4 us: far_term(): jnp.einsum('sbn,krn->skbr', source_row, left, preferred_element_type=jnp....]
    pallas_call x0 -> x1, Pallas kernels: none -> 42 us  [local(): pl.pallas_call(functools.partial(kernel, dims), out_shape=jax.ShapeDtypeS...]
    all_gather x1 -> x0, waiting for transfers between devices: 24.7 us -> none  [local(): gathered = lax.all_gather(sources, 'row', axis=0, tiled=True)]
    unnamed x4 -> x2, local copies, waits for them, and re-layouts: 0.01 us -> 3.01 us
    while x224 -> x0, local copies, waits for them, and re-layouts: 2.89 us -> none
  transfers between devices with their start and end apart: 19 -> 0, of which waited for: 17 -> 0; matrix products, arithmetic and copies ran while one was open for 4% -> 0% of each run, Pallas kernels for 0% -> 0%
where the time goes in v1:
time: 45.2 us; the launch traced here: 45 us
  Pallas kernels  42 us (93%)
  local copies, waits for them, and re-layouts  3.01 us (7%)
    pallas_call x1, Pallas kernels, local(): pl.pallas_call(functools.partial(kernel, dims), out_shape=jax.ShapeDtypeS...  42 us
    unnamed x2, local copies, waits for them, and re-layouts  3.01 us

profile of v1, /device:TPU:0, one launch (start us, length us, event | category | flops | bytes accessed | tf_op | source)
XLA Modules:
  0.0 45.0 jit_solution(5454749385043469288)
XLA Ops:
  0.0 1.3 %copy.7.offsets = s32[3,2]{1,0:T(4,128)} copy(s32[3,2]{0,1:T(2,128)} %param.11) | data formatting | bytes 48 | tf_op args[5]
  1.3 42.0 %shard_map.64 = f32[64,1024]{1,0:T(8,128)} custom-call(bf16[64,1024]{1,0:T(8,128)(2,1)} %bitcast.7, bf16[2,720,1024]{2,1,0:T(8,128)(2,1)} %bitcast.5, bf16[2,720,1024]{2,1,0:T(8,128)(2,1)} %bitcast.6, bf16[3,1024,1024]{2,1,0:T(8,128)(2,1)} %near_hbm.1, s32[2,15]{1,0:T(2,128)} %ranks.1, s32[3,2]{1,0:T(4,128)} %copy.7.offsets), custom_call_target="tpu_custom_call" | custom-call | flops 3623878656 | bytes 13000000 | tf_op jit(solution)/shard_map/pallas_call | solution.py:355
  43.3 1.7 %copy.9 = f32[1,8,8,1024]{3,2,1,0:T(8,128)} copy(f32[1,8,8,1024]{3,2,1,0:T(8,128)} %bitcast.4) | data formatting | bytes 524288

commit v2 on v1

--- a/solution.py
+++ b/solution.py
@@ -8,6 +8,8 @@
 from jax.sharding import PartitionSpec as P
 
 MESH = pl.DeviceIdType.MESH
+PARTS = 4
+ORDER = ((0, 1, 2, 3), (2, 3, 0, 1))
 F32 = jnp.float32
 BF16 = jnp.bfloat16
 LANES = 128
@@ -25,7 +27,7 @@
     chips = count // 2
     half_ring = chips // 2
     rows = ecol * beams
-    half = rows // 2
+    half = rows // PARTS
     used = slots * rank
 
     me = lax.axis_index("row")
@@ -65,34 +67,34 @@
     loads[0].start()
     loads[1].start()
     loads[3].start()
+    loads[2].start()
+    loads[4].start()
+    loads[5].start()
     pl.semaphore_wait(barrier, 3)
 
     def part(ref, lead, h):
         return ref.at[lead, pl.ds(h * half, half)]
 
-    def hop(way, step, h, row, source=None):
+    def hop(way, step, h, row):
         block = part(rows_all, row, h)
         return send(
-            block if source is None else source, block,
+            block, block,
             g_send.at[way, step - 1, h], g_recv.at[way, step - 1, h],
             ahead if way == 0 else behind,
         )
 
-    def cross(index, h, row, source=None):
+    def cross(index, h, row):
         block = part(rows_all, row, h)
         return send(
-            block if source is None else source, block,
-            gs_send.at[index, h], gs_recv.at[index, h], sibling,
+            block, block, gs_send.at[index, h], gs_recv.at[index, h], sibling,
         )
 
-    for h in range(2):
-        mine = src.at[pl.ds(h * half, half)]
-        hop(0, 1, h, me, mine).start()
-        hop(1, 1, h, me, mine).start()
-        cross(0, h, me, mine).start()
-    loads[2].start()
-    loads[4].start()
-    loads[5].start()
+    loads[0].wait()
+    for i in range(PARTS):
+        for way in range(2):
+            hop(way, 1, ORDER[way][i], me).start()
+    for h in range(PARTS):
+        cross(0, h, me).start()
 
     for w in range(2):
         left[w, pl.ds(used, depth - used), :] = jnp.zeros((depth - used, width), BF16)
@@ -106,8 +108,8 @@
         for k in range(slots):
             free = jnp.int32(1)
             for n in range(nnear):
-                rows_off = offsets[n, 0] - (me - count * w)
-                cols_off = offsets[n, 1] - (k - (ecol - 1))
+                rows_off = offsets[0, n] - (me - count * w)
+                cols_off = offsets[1, n] - (k - (ecol - 1))
                 free = free * jnp.minimum(rows_off * rows_off + cols_off * cols_off, 1)
             level = rank * k + ranks[w, k] * free
             top = jnp.where(lane >= rank * k, level, top)
@@ -152,18 +154,19 @@
                 spread_all[target, :, pl.ds(low, LANES)] = value.astype(BF16)
 
     def take(step, all_on):
-        for h in range(2):
+        for i in range(PARTS):
             for way in range(2):
+                h = ORDER[way][i]
                 row = row_at(pos - step if way == 0 else pos + step)
                 index = chips - step if way == 0 else step
                 hop(way, step, h, row).wait_recv()
-                if all_on or h == way:
+                if all_on or 2 * i < PARTS:
                     hop(way, step + 1, h, row).start()
                 cross(index, h, row).start()
 
     def cross_arrived(index, place):
         other = 2 * chip_at(place) + 1 - core
-        for h in range(2):
+        for h in range(PARTS):
             cross(index, h, other).wait_recv()
 
     def both_coeffs(step):
@@ -177,25 +180,23 @@
     def gather_step(step, carry):
         take(step, True)
 
-        @pl.when(step == 1)
-        def _():
-            loads[0].wait()
-            loads[1].wait()
-            loads[3].wait()
-            cross_arrived(0, pos)
-            coeffs_of(pos)
-
         @pl.when(step > 1)
         def _():
             both_coeffs(step - 1)
         return carry
 
+    loads[1].wait()
+    loads[3].wait()
+    cross_arrived(0, pos)
+    coeffs_of(pos)
     lax.fori_loop(1, half_ring - 1, gather_step, 0)
     take(half_ring - 1, False)
     both_coeffs(half_ring - 2)
-    for way in range(2):
-        hop(way, half_ring, way, row_at(pos + half_ring)).wait_recv()
-        cross(half_ring, way, row_at(pos + half_ring)).start()
+    for i in range(PARTS // 2):
+        for way in range(2):
+            h = ORDER[way][i]
+            hop(way, half_ring, h, row_at(pos + half_ring)).wait_recv()
+            cross(half_ring, h, row_at(pos + half_ring)).start()
     both_coeffs(half_ring - 1)
     cross_arrived(half_ring, pos + half_ring)
     coeffs_of(pos + half_ring)
@@ -252,37 +253,37 @@
         ring_out[way, step - 1, at, :] = total.astype(ring_out.dtype)
         ring(way, step, h).start()
 
+    def pass_all(step, turns, fresh):
+        for i in turns:
+            for way in range(2):
+                pass_on(step, way, ORDER[way][i], fresh)
+
     loads[2].wait()
     loads[4].wait()
     fields_of(half_ring)
     both_fields(half_ring - 1)
     cross_sum(half_ring).wait_recv()
-    pass_on(1, 0, 0, True)
-    pass_on(1, 1, 1, True)
+    pass_all(1, (0, 1), True)
     cross_sum(half_ring - 1).wait_recv()
     cross_sum(chips - half_ring + 1).wait_recv()
-    pass_on(2, 0, 1, True)
-    pass_on(2, 1, 0, True)
-    both_fields(half_ring - 2)
-    pass_on(2, 0, 0, False)
-    pass_on(2, 1, 1, False)
+    pass_all(2, (2, 3), True)
+
+    def more_fields(step, carry):
+        both_fields(half_ring - step)
+        return carry
+
+    lax.fori_loop(2, half_ring, more_fields, 0)
+    fields_of(0)
+    pass_all(2, (0, 1), False)
 
     def reduce_step(step, carry):
-        distance = half_ring - step
-
-        @pl.when(distance > 0)
-        def _():
-            both_fields(distance)
-        cross_sum(distance + 1).wait_recv()
-        cross_sum(chips - distance - 1).wait_recv()
-        pass_on(step, 0, 1, False)
-        pass_on(step, 1, 0, False)
-        pass_on(step, 0, 0, False)
-        pass_on(step, 1, 1, False)
+        distance = half_ring - step + 1
+        cross_sum(distance).wait_recv()
+        cross_sum(chips - distance).wait_recv()
+        pass_all(step, (2, 3, 0, 1), False)
         return carry
 
     lax.fori_loop(3, half_ring + 1, reduce_step, 0)
-    fields_of(0)
 
     loads[5].wait()
     for i in range(3):
@@ -300,8 +301,8 @@
                 ((square - offset) // 2).astype(F32)]
 
     def near_step(n, carry):
-        by_row = weights(offsets[n, 0])
-        by_col = weights(offsets[n, 1])
+        by_row = weights(offsets[0, n])
+        by_col = weights(offsets[1, n])
         picked = sum(beside[i] * by_row[i] for i in range(3))
         shifted = sum(
             picked[i * beams:i * beams + rows, :] * by_col[i] for i in range(3)).astype(BF16)
@@ -311,7 +312,7 @@
     lax.fori_loop(0, nnear, near_step, 0)
 
     cross_sum(0).wait_recv()
-    for h in range(2):
+    for h in range(PARTS):
         at = pl.ds(h * half, half)
         total = near_acc[at, :] + own(0, h)
         for way in range(2):
@@ -321,18 +322,19 @@
 
     def sent(step, carry):
         for way in range(2):
-            for h in range(2):
+            for h in range(PARTS):
                 hop(way, step, h, me).wait_send()
                 ring(way, half_ring + 1 - step, h).wait_send()
         return carry
 
     lax.fori_loop(1, half_ring, sent, 0)
     for way in range(2):
-        hop(way, half_ring, way, me).wait_send()
-        ring(way, 1, way).wait_send()
+        for h in ORDER[way][:PARTS // 2]:
+            hop(way, half_ring, h, me).wait_send()
+            ring(way, 1, h).wait_send()
 
     def crossed(index, carry):
-        for h in range(2):
+        for h in range(PARTS):
             cross(index, h, me).wait_send()
         cross_sum(index).wait_send()
         return carry
@@ -372,12 +374,12 @@
             pltpu.VMEM((2, 8, depth), F32),
             pltpu.VMEM((rows, width), F32),
             dma((6,)),
-            dma((2, half_ring, 2)),
-            dma((2, half_ring, 2)),
-            dma((chips, 2)),
-            dma((chips, 2)),
-            dma((2, half_ring, 2)),
-            dma((2, half_ring, 2)),
+            dma((2, half_ring, PARTS)),
+            dma((2, half_ring, PARTS)),
+            dma((chips, PARTS)),
+            dma((chips, PARTS)),
+            dma((2, half_ring, PARTS)),
+            dma((2, half_ring, PARTS)),
             dma((chips,)),
             dma((chips,)),
         ],
@@ -389,7 +391,7 @@
         sources.reshape(rows, width),
         far_left.reshape(2, slots * rank, width),
         far_right.reshape(2, slots * rank, width),
-        near_blocks, ranks, near_offsets,
+        near_blocks, ranks, near_offsets.T,
     )
     return fields.reshape(1, ecol, beams, width)
 

time: 45.2 us -> 40.1 us (0.89)
  Pallas kernels: 42 us -> 38.2 us
  local copies, waits for them, and re-layouts: 3.01 us -> 1.67 us
    pallas_call x1, Pallas kernels: 42 us -> 38.2 us  [local(): pl.pallas_call(functools.partial(kernel, dims), out_shape=jax.ShapeDtypeS...]
    unnamed x2 -> x1, local copies, waits for them, and re-layouts: 3.01 us -> 1.67 us
where the time goes in v2:
time: 40.1 us; the launch traced here: 39.9 us
  Pallas kernels  38.2 us (95%)
  local copies, waits for them, and re-layouts  1.67 us (4%)
    pallas_call x1, Pallas kernels, local(): pl.pallas_call(functools.partial(kernel, dims), out_shape=jax.ShapeDtypeS...  38.2 us
    unnamed x1, local copies, waits for them, and re-layouts  1.67 us

profile of v2, /device:TPU:0, one launch (start us, length us, event | category | flops | bytes accessed | tf_op | source)
XLA Modules:
  0.0 39.9 jit_solution(14041868154002843542)
XLA Ops:
  0.0 38.2 %shard_map.64 = f32[64,1024]{1,0:T(8,128)} custom-call(bf16[64,1024]{1,0:T(8,128)(2,1)} %bitcast.8, bf16[2,720,1024]{2,1,0:T(8,128)(2,1)} %bitcast.6, bf16[2,720,1024]{2,1,0:T(8,128)(2,1)} %bitcast.7, bf16[3,1024,1024]{2,1,0:T(8,128)(2,1)} %near_hbm.1, s32[2,15]{1,0:T(2,128)} %ranks.1, s32[2,3]{1,0:T(2,128)} %bitcast.9), custom_call_target="tpu_custom_call" | custom-call | flops 3623878656 | bytes 13000000 | tf_op jit(solution)/shard_map/pallas_call | solution.py:357
  38.3 1.7 %copy.8 = f32[1,8,8,1024]{3,2,1,0:T(8,128)} copy(f32[1,8,8,1024]{3,2,1,0:T(8,128)} %bitcast.5) | data formatting | bytes 524288
